TPU v7x, 512 devices: a whole 4x4x16 slice. The times are simulated.
512 devices in a mesh: users: 32 (over z, core), hist: 16 (over x, y).
Axes of the slice: x: 4, y: 4, z: 16, core: 2. Of those that a mesh axis runs over, the one named last changes fastest.
Arguments:
- item_table: bfloat16 [8192, 1024], P('users'), may hold values from -40 to 40
- cand_owner: int32 [32, 768, 1], P('users', 'hist'), may hold values from 0 to 31; in each aligned block of 48 rows (0 to 47, 48 to 95, ..., all dimensions but the last counted through in order) at most 3 rows name the same one
- cand_row: int32 [32, 768], P('users', 'hist'), may hold values from 0 to 255
- counts: int32 [32], P('users'), may hold values from 1 to 768, 15360 in all
- hist_keys: bfloat16 [32, 8192, 1024], P('users', 'hist'), may hold values from -6 to 6
- hist_values: bfloat16 [32, 8192, 1024], P('users', 'hist'), may hold values from -25 to 25
- gain_in: float32 [1024], replicated, may hold values from 0.25 to 1.75
- w_in: bfloat16 [1024, 2048], P('hist'), may hold values from -0.1875 to 0.1875
- bias_in: float32 [2048], replicated, may hold values from -3 to 3
- gain_mid: float32 [1024], replicated, may hold values from 0.25 to 1.75
- w_out: bfloat16 [1024, 1024], P('hist'), may hold values from -0.1875 to 0.1875
Outputs:
- ranked: bfloat16 [32, 768, 1024], P('users', 'hist')
Inputs may be any that keep to these rules, and one draw needn't show every extreme that they name: `cand_owner`: in each aligned block of 48 candidates (the candidates of one device), no table shard is named more than 3 times, and one shard exactly 3 times in some blocks. The live candidates of a user are its first counts[u] slots; some user has all 768.
All inputs are finite; a program needn't handle non-finite values. No bound on the sum of `counts` on one device may be relied on, other than what follows from the above.
Results may differ from a plain program's by a relative error of at most 0.0045.
Values may be sent and summed in bfloat16 or wider, within the bound.
A program may use at most 64 MiB of HBM per device.

v0:
```python
import jax
import jax.numpy as jnp
from jax import lax
from jax.sharding import PartitionSpec as P

HEADS = 8


eps = 1e-05


def layer_norm(values, gain):
    mean = jnp.mean(values, axis=-1, keepdims=True)
    centred = values - mean
    spread = jnp.mean(centred * centred, axis=-1, keepdims=True)
    return centred * lax.rsqrt(spread + eps) * gain


def slot_plan(owners, rows_local, slot_count, user_count):
    blocks, width = owners.shape
    same = owners[:, :, None] == owners[:, None, :]
    earlier = jnp.arange(width)[None, :, None] > jnp.arange(width)[None, None, :]
    rank = jnp.sum(jnp.logical_and(same, earlier), axis=2)
    block_index = jnp.arange(blocks, dtype=jnp.int32)[:, None]
    position = (owners * (blocks * slot_count) + block_index * slot_count + rank).reshape(-1)
    requests = (
        jnp.zeros((user_count * blocks * slot_count,), jnp.int32)
        .at[position]
        .set(rows_local.reshape(-1))
    )
    return (requests.reshape(user_count, blocks * slot_count), position)


def local(
    item_table,
    cand_owner,
    cand_row,
    counts,
    hist_keys,
    hist_values,
    gain_in,
    w_in,
    bias_in,
    gain_mid,
    w_out,
):
    width = item_table.shape[1]
    head_size = width // HEADS
    user_count = lax.axis_size("users")
    cand_local = cand_owner.shape[1]
    slot_count = max(2, (2 * cand_local + user_count - 1) // user_count)
    hist_index = lax.axis_index("hist")
    live = counts[0]
    requests, position = slot_plan(cand_owner[:, :, 0], cand_row, slot_count, user_count)
    looked = jnp.take(
        item_table,
        lax.all_to_all(requests, "users", split_axis=0, concat_axis=0, tiled=True),
        axis=0,
    )
    returned = lax.all_to_all(looked, "users", split_axis=0, concat_axis=0, tiled=True)
    fetched = jnp.take(returned.reshape(-1, width), position, axis=0)
    normed = layer_norm(fetched.astype(jnp.float32), gain_in).astype(jnp.bfloat16)
    columns = normed
    projected = jnp.dot(
        columns,
        lax.all_gather(w_in, "hist", axis=0, tiled=True),
        preferred_element_type=jnp.float32,
    )
    activated = jax.nn.silu(projected + bias_in).astype(jnp.bfloat16)
    queries_all = lax.all_gather(activated[:, width:], "hist", axis=0, tiled=True)
    gate_rows = activated[:, :width]
    keys_local = hist_keys[0]
    values_local = hist_values[0]
    score_scale = head_size ** (-0.5)
    outputs = []
    for head_index in range(HEADS):
        first = head_index * head_size
        scores = (
            jnp.einsum(
                "qd,kd->qk",
                queries_all[:, first : first + head_size],
                keys_local[:, first : first + head_size],
                preferred_element_type=jnp.float32,
            )
            * score_scale
        )
        weights = jax.nn.silu(scores).astype(jnp.bfloat16)
        outputs.append(
            jnp.dot(
                weights,
                values_local[:, first : first + head_size],
                preferred_element_type=jnp.float32,
            )
        )
    attended = lax.psum_scatter(
        jnp.concatenate(outputs, axis=1), "hist", scatter_dimension=0, tiled=True
    )
    gated = (layer_norm(attended, gain_mid) * gate_rows.astype(jnp.float32)).astype(jnp.bfloat16)
    columns = gated
    mixed = jnp.dot(
        columns,
        lax.all_gather(w_out, "hist", axis=0, tiled=True),
        preferred_element_type=jnp.float32,
    )
    mixed = mixed + fetched.astype(jnp.float32)
    row_index = hist_index * cand_local + jnp.arange(cand_local, dtype=jnp.int32)
    result = jnp.where((row_index < live)[:, None], mixed, 0.0).astype(jnp.bfloat16)
    return result[None]


def solution(mesh):
    placed = (
        P("users", None),
        P("users", "hist", None),
        P("users", "hist"),
        P("users"),
        P("users", "hist", None),
        P("users", "hist", None),
        P(),
        P("hist", None),
        P(),
        P(),
        P("hist", None),
    )
    return jax.shard_map(
        local, mesh=mesh, in_specs=placed, out_specs=P("users", "hist", None), check_vma=False
    )
```

profile of v0, /device:TPU:1, one launch (start us, length us, event | category | flops | bytes accessed | tf_op | source)
XLA Modules:
  0.0 326.7 jit_solution(515576095392178971)
XLA Ops:
  6.5 0.0 copy-start
  6.5 0.0 all-gather.4.cloned.1.call-start
  6.5 0.7 all-gather.4.cloned.1.call-update
  7.3 0.9 convert_reduce_fusion.1
  8.2 0.7 fusion.73
  8.8 0.9 scatter_custom_fusion
  9.7 0.1 all_to_all.13
  9.8 28.3 %all_to_all.20 = s32[32,1,3]{2,1,0:T(1,128)S(1)} all-to-all(s32[32,1,3]{2,1,0:T(1,128)S(1)} %bitcast.28), channel_id=1, replica_groups=mesh['users'=32,'hist'=16] {'users'}, dimensions={0} | all-to-all | bytes 768 | tf_op jit(solution)/shard_map/all_to_all | solution.py:57
  38.1 0.1 copy.52
  38.2 0.1 copy.53
  38.3 0.1 reshape.215
  38.4 0.0 copy-done
  38.5 0.0 copy-start.6
  38.5 0.8 gather_fusion
  39.2 0.0 copy-start.4
  39.3 0.0 copy-start.5
  39.3 0.1 reshape.214
  39.4 0.1 copy.50
  39.5 0.1 copy.51
  39.6 0.9 broadcast_select_fusion
  40.5 4.4 %all-to-all-start.1 = ((bf16[32,3,1024]{2,1,0:T(4,128)(2,1)}), bf16[32,3,1024]{2,1,0:T(4,128)(2,1)S(1)}, u32[]{:S(2)}, u32[]{:S(2)}) async-start(bf16[32,3,1024]{2,1,0:T(4,128)(2,1)} %broadcast_select_fusion), calls=%async_computation.1 | async-start | bytes 524288 | tf_op jit(solution)/shard_map/all_to_all | solution.py:60
  44.9 0.0 all-gather.6.cloned.1.call-start
  45.0 0.0 copy-done.6
  45.0 21.9 %all-to-all-done.1 = bf16[32,3,1024]{2,1,0:T(4,128)(2,1)S(1)} async-done(((bf16[32,3,1024]{2,1,0:T(4,128)(2,1)}), bf16[32,3,1024]{2,1,0:T(4,128)(2,1)S(1)}, u32[]{:S(2)}, u32[]{:S(2)}) %all-to-all-start.1) | async-done | bytes 196640 | tf_op jit(solution)/shard_map/all_to_all | solution.py:60
  67.0 0.2 reshape.212
  67.1 0.7 gather_fusion.1
  67.8 0.2 convert_reduce_fusion
  68.0 0.2 fusion.21
  68.2 0.0 copy-start.3
  68.2 14.3 %all-gather.4.cloned.1.call-done = bf16[1024,2048]{1,0:T(8,128)(2,1)} async-done(((bf16[64,2048]{1,0:T(8,128)(2,1)}), bf16[1024,2048]{1,0:T(8,128)(2,1)}) %all-gather.4.cloned.1.call-update) | async-done | bytes 4194320 | tf_op jit(solution)/shard_map/all_gather | solution.py:66
  82.6 0.0 copy-done.4
  82.6 0.0 copy-done.5
  82.6 3.1 multiply_convert_fusion.8
  85.7 0.6 slice.108
  86.3 0.0 all-gather.6.cloned.1.call-update
  86.3 0.0 reduce-scatter.2.cloned.1.call-start
  86.4 58.2 %all-gather.6.cloned.1.call-done = bf16[768,1024]{1,0:T(8,128)(2,1)} async-done(((bf16[48,1024]{1,0:T(8,128)(2,1)}), bf16[768,1024]{1,0:T(8,128)(2,1)}) %all-gather.6.cloned.1.call-update) | async-done | bytes 1572880 | tf_op jit(solution)/shard_map/all_gather | solution.py:70
  144.6 0.0 copy-done.3
  144.6 0.0 copy-start.2
  144.6 2.6 convolution_dynamic-update-slice_fusion.7
  147.2 0.0 copy-done.2
  147.2 2.4 convolution_dynamic-update-slice_fusion.6
  149.6 2.4 convolution_dynamic-update-slice_fusion.5
  152.0 2.4 convolution_dynamic-update-slice_fusion.4
  154.4 2.4 convolution_dynamic-update-slice_fusion.3
  156.8 2.4 convolution_dynamic-update-slice_fusion.2
  159.2 2.4 convolution_dynamic-update-slice_fusion.1
  161.5 2.4 convolution_dynamic-update-slice_fusion
  163.9 0.0 copy-start.1
  163.9 0.0 reduce-scatter.2.cloned.1.call-update
  163.9 0.0 all-gather.8.cloned.1.call-start
  164.0 0.5 all-gather.8.cloned.1.call-update
  165.2 88.8 %reduce-scatter.2.cloned.1.call-done = f32[48,1024]{1,0:T(8,128)} async-done(((f32[768,1024]{1,0:T(8,128)}), f32[48,1024]{1,0:T(8,128)}) %reduce-scatter.2.cloned.1.call-update) | async-done | bytes 196624 | tf_op jit(solution)/shard_map/reduce_scatter | solution.py:95
  254.0 1.0 reduce_sum.51
  255.0 1.1 multiply_reduce_fusion
  256.1 61.2 %all-gather.8.cloned.1.call-done = bf16[1024,1024]{1,0:T(8,128)(2,1)} async-done(((bf16[64,1024]{1,0:T(8,128)(2,1)}), bf16[1024,1024]{1,0:T(8,128)(2,1)}) %all-gather.8.cloned.1.call-update) | async-done | bytes 2097168 | tf_op jit(solution)/shard_map/all_gather | solution.py:102
  317.3 0.0 copy-done.1
  317.3 2.9 fusion.2
  (10 shorter events, 0.1 us)
Async XLA Ops:
  6.5 31.9 %copy-start = (bf16[256,1024]{1,0:T(8,128)(2,1)S(1)}, bf16[256,1024]{1,0:T(8,128)(2,1)}, u32[]{:S(2)}) copy-start(bf16[256,1024]{1,0:T(8,128)(2,1)} %param.11) | copy-start | bytes 1572868
  6.5 76.0 %all-gather.4.cloned.1.call-start = ((), (), s32[]{:S(2)}) async-start(), calls=%async_computation.3 | async-start | bytes 4456448 | tf_op jit(solution)/shard_map/all_gather | solution.py:66
  38.5 6.6 %copy-start.6 = (s32[1,48,1]{1,2,0:T(1,128)S(1)}, s32[1,48,1]{1,2,0:T(1,128)}, u32[]{:S(2)}) copy-start(s32[1,48,1]{1,2,0:T(1,128)} %param.12) | copy-start | bytes 580
  39.2 43.3 %copy-start.4 = (f32[2048]{0:T(1024)S(1)}, f32[2048]{0:T(1024)}, u32[]{:S(2)}) copy-start(f32[2048]{0:T(1024)} %param.19) | copy-start | bytes 24580
  39.3 43.3 %copy-start.5 = (f32[1024]{0:T(1024)S(1)}, f32[1024]{0:T(1024)}, u32[]{:S(2)}) copy-start(f32[1024]{0:T(1024)} %param.17) | copy-start | bytes 12292
  40.5 26.4 %all-to-all-start.1 = ((bf16[32,3,1024]{2,1,0:T(4,128)(2,1)}), bf16[32,3,1024]{2,1,0:T(4,128)(2,1)S(1)}, u32[]{:S(2)}, u32[]{:S(2)}) async-start(bf16[32,3,1024]{2,1,0:T(4,128)(2,1)} %broadcast_select_fusion), calls=%async_computation.1 | async-start | bytes 524288 | tf_op jit(solution)/shard_map/all_to_all | solution.py:60
  44.9 99.7 %all-gather.6.cloned.1.call-start = ((), (), s32[]{:S(2)}) async-start(), calls=%async_computation.4 | async-start | bytes 1671168 | tf_op jit(solution)/shard_map/all_gather | solution.py:70
  68.2 76.4 %copy-start.3 = (bf16[1,512,1024]{2,1,0:T(8,128)(2,1)S(1)}, bf16[1,512,1024]{2,1,0:T(8,128)(2,1)}, u32[]{:S(2)}) copy-start(bf16[1,512,1024]{2,1,0:T(8,128)(2,1)} %param.16) | copy-start | bytes 3145732
  86.3 167.6 %reduce-scatter.2.cloned.1.call-start = ((), (), s32[]{:S(2)}) async-start(), calls=%async_computation.5 | async-start | bytes 3342336 | tf_op jit(solution)/shard_map/reduce_scatter | solution.py:95
  144.6 2.6 copy-start.2
  163.9 153.4 %copy-start.1 = (f32[1024]{0:T(1024)S(1)}, f32[1024]{0:T(1024)}, u32[]{:S(2)}) copy-start(f32[1024]{0:T(1024)} %param.20) | copy-start | bytes 12292
  163.9 153.4 %all-gather.8.cloned.1.call-start = ((), (), s32[]{:S(2)}) async-start(), calls=%async_computation.6 | async-start | bytes 2228224 | tf_op jit(solution)/shard_map/all_gather | solution.py:102
Sparse Core Ops, SparseCore 0:
  10.4 72.1 all-gather.3
  86.5 58.0 all-gather.5
  164.1 89.8 reduce-scatter.1
  256.8 60.4 all-gather.7
where the time goes:
time: 327 us
  waiting for transfers between devices  246 us (75%)
  blocking collectives  28.3 us (9%)
  matrix products  25.3 us (8%)
  between operations  13.9 us (4%)
  other arithmetic  5.12 us (2%)
  starting transfers between devices  4.56 us (1%)
  local copies, waits for them, and re-layouts  3.84 us (1%)
    reduce_scatter x1, waiting for transfers between devices, local(): lax.psum_scatter(jnp.concatenate(outputs, axis=1), 'hist', scatter_dimens...  88.8 us
    all_gather x1, waiting for transfers between devices, local(): lax.all_gather(w_out, 'hist', axis=0, tiled=True)  61.2 us
    all_gather x1, waiting for transfers between devices, local(): lax.all_gather(activated[:, width:], 'hist', axis=0, tiled=True)  58.2 us
    all_to_all x1, blocking collectives, local(): lax.all_to_all(requests, 'users', split_axis=0, concat_axis=0, tiled=True)  28.3 us
    all_to_all x1, waiting for transfers between devices, local(): lax.all_to_all(looked, 'users', split_axis=0, concat_axis=0, tiled=True)  21.9 us
    dot_general x8, matrix products, local(): jnp.dot(weights, values_local[:, first:first + head_size], preferred_elem...  19.3 us
    all_gather x1, waiting for transfers between devices, local(): lax.all_gather(w_in, 'hist', axis=0, tiled=True)  14.3 us
  transfers between devices with their start and end apart: 5, of which 5 were waited for; matrix products, arithmetic and copies ran while one was open for 3% of the time, Pallas kernels for 0%

commit v1 on v0

v1 whole, which is shorter than its diff:
```python
import functools

import jax
import jax.numpy as jnp
from jax import lax
from jax.experimental import pallas as pl
from jax.experimental.pallas import tpu as pltpu
from jax.sharding import PartitionSpec as P

MESH = pl.DeviceIdType.MESH
F32, BF16 = jnp.float32, jnp.bfloat16

HEADS = 8
HEAD = 128
D = 1024
HALF = D // 2
QUARTER = D // 4
CAND = 48
ROWS = 256
PLANES = 16
SIDE = 4
SHARD = D // (SIDE * SIDE)
SLOTS = 6
PIECES = 8
MESSAGE = SLOTS * PIECES
EPS = 1e-05
MESSAGES = 160

GROUPS = ((1, 15, 2, 14), (3, 13, 4, 12), (5, 11, 6, 10), (7, 9, 8, 0))


def norm(values, gain):
    mean = jnp.mean(values, axis=-1, keepdims=True)
    centred = values - mean
    spread = jnp.mean(centred * centred, axis=-1, keepdims=True)
    return centred * lax.rsqrt(spread + EPS) * gain


def silu(values):
    half = values * 0.5
    return half + half * jnp.tanh(half)


def kernel(
    table_ref,
    owner_row_ref,
    row_row_ref,
    counts_ref,
    keys_ref,
    values_ref,
    gain_in_ref,
    w_in_ref,
    bias_ref,
    gain_mid_ref,
    w_out_ref,
    out_ref,
    table,
    keys,
    values,
    wq,
    wr,
    plan,
    asked,
    served,
    rows,
    fetched,
    normed,
    gates,
    queries,
    own,
    part_out,
    part_in,
    sum_out,
    sum_in,
    send_sem,
    recv_sem,
    local_sem,
):
    users, hist = lax.axis_index("users"), lax.axis_index("hist")
    z, c = users // 2, lax.rem(users, 2)
    x, y = hist // SIDE, lax.rem(hist, SIDE)

    def at_z(step):
        return (lax.rem(z + step, PLANES) * 2 + c, hist)

    def at_axis(axis, step):
        if axis == "x":
            return (users, lax.rem(x + step, SIDE) * SIDE + y)
        return (users, x * SIDE + lax.rem(y + step, SIDE))

    partner = (z * 2 + 1 - c, hist)
    started = []

    def send(src, dst, device):
        index = len(started)
        copy = pltpu.make_async_remote_copy(
            src_ref=src,
            dst_ref=dst,
            send_sem=send_sem.at[index],
            recv_sem=recv_sem.at[index],
            device_id=device,
            device_id_type=MESH,
        )
        copy.start()
        started.append(copy)
        return copy

    barrier = pltpu.get_barrier_semaphore()
    peers = [at_z(step) for step in range(1, PLANES)] + [partner]
    peers += [at_axis(axis, step) for axis in "xy" for step in range(1, SIDE)]
    for peer in peers:
        pl.semaphore_signal(barrier, inc=1, device_id=peer, device_id_type=MESH)

    locals_ = []

    def load(src, dst):
        copy = pltpu.make_async_copy(src, dst, local_sem.at[len(locals_)])
        copy.start()
        locals_.append(copy)
        return copy

    load_q, load_r = [], []
    for core in range(2):
        for half in range(2):
            first = (core * 2 + half) * QUARTER
            load_q.append(load(w_in_ref.at[:, pl.ds(D + first, QUARTER)], wq.at[core, half, x, y]))
    load_table = load(table_ref, table.at[c])
    for core in range(2):
        for half in range(2):
            first = (core * 2 + half) * QUARTER
            mine = wr.at[core, half, x, y]
            load_r.append(load(w_in_ref.at[:, pl.ds(first, QUARTER)], mine.at[:, pl.ds(0, QUARTER)]))
            load_r.append(
                load(w_out_ref.at[:, pl.ds(first, QUARTER)], mine.at[:, pl.ds(QUARTER, QUARTER)])
            )
    load_keys = load(keys_ref, keys)
    load_values = load(values_ref, values)

    chip_row = ((owner_row_ref[...] >> 1) - z) & (PLANES - 1)
    later = lax.broadcasted_iota(jnp.int32, (CAND, CAND), 0)
    earlier = lax.broadcasted_iota(jnp.int32, (CAND, CAND), 1)
    chip_col = jnp.where(earlier == later, chip_row.astype(F32), 0.0)
    chip_col = jnp.sum(chip_col, axis=1, keepdims=True).astype(jnp.int32)
    before = earlier < later
    same = jnp.where((chip_col == chip_row) & before, 1.0, 0.0)
    rank = jnp.sum(same, axis=1, keepdims=True).astype(jnp.int32)
    lane = lax.broadcasted_iota(jnp.int32, (CAND, 128), 1) & 63
    slot_of = jnp.where((lane >> 3 == rank) & (lane < MESSAGE), 1.0, 0.0).astype(BF16)
    chip_of = chip_row == lax.broadcasted_iota(jnp.int32, (PLANES, CAND), 0)
    row_part = jnp.where(chip_of, row_row_ref[...].astype(F32), 0.0).astype(BF16)
    core_part = jnp.where(chip_of, ((owner_row_ref[...] & 1) + 1).astype(F32), 0.0).astype(BF16)
    wanted = jnp.dot(row_part, slot_of, preferred_element_type=F32)
    wanted += (jnp.dot(core_part, slot_of, preferred_element_type=F32) - 1.0) * ROWS
    wanted = wanted.astype(jnp.int32)
    for step in range(PLANES):
        plan[step] = wanted[step : step + 1]
    asked[0] = wanted[0:1]

    for copy in load_q:
        copy.wait()
    pl.semaphore_wait(barrier, len(peers))

    share_table = send(table_ref, table.at[c], partner)
    asks = {}
    for step in (8, 7, 9, 6, 10, 5, 11, 4, 12, 3, 13, 2, 14, 1, 15):
        asks[PLANES - step] = send(plan.at[step], asked.at[PLANES - step], at_z(step))

    axes = (("y", "x"), ("x", "y"))

    def block(buffer, half, outer, inner):
        if half == 0:
            return buffer.at[c, 0, lax.rem(x + outer, SIDE), lax.rem(y + inner, SIDE)]
        return buffer.at[c, 1, lax.rem(x + inner, SIDE), lax.rem(y + outer, SIDE)]

    def group(buffer, half, outer, first, count):
        if half == 0:
            return buffer.at[c, 0, lax.rem(x + outer, SIDE), pl.ds(first, count)]
        return buffer.at[c, 1, pl.ds(first, count), lax.rem(y + outer, SIDE)]

    def weight_inner(buffer, half):
        mine = block(buffer, half, 0, 0)
        return [send(mine, mine, at_axis(axes[half][0], step)) for step in (2, 1, 3)]

    def weight_outer(buffer, half):
        low, high = group(buffer, half, 0, 0, 2), group(buffer, half, 0, 2, 2)
        axis = axes[half][1]
        return {
            "low_up": send(low, low, at_axis(axis, 1)),
            "high_down": send(high, high, at_axis(axis, 3)),
            "high_up": send(high, high, at_axis(axis, 1)),
            "low_down": send(low, low, at_axis(axis, 3)),
        }

    def weight_relay(buffer, half, first_hop):
        axis = axes[half][1]
        first_hop["low_up"].wait_recv()
        low = group(buffer, half, 3, 0, 2)
        up = send(low, low, at_axis(axis, 1))
        first_hop["high_down"].wait_recv()
        high = group(buffer, half, 1, 2, 2)
        return up, send(high, high, at_axis(axis, 3))

    def share(ref):
        return send(ref, ref, partner)

    shared_q, shared_r = [], []
    inner_q = [weight_inner(wq, half) for half in range(2)]
    for half in range(2):
        for copy in inner_q[half]:
            copy.wait_recv()
    outer_q = [weight_outer(wq, half) for half in range(2)]
    for copy in load_r:
        copy.wait()
    inner_r = [weight_inner(wr, half) for half in range(2)]
    for half in range(2):
        shared_q += [share(block(wq, half, 0, inner)) for inner in range(1, SIDE)]

    load_table.wait()
    share_table.wait_recv()
    lanes = lax.broadcasted_iota(jnp.int32, (1, 128), 1)
    items = lax.broadcasted_iota(jnp.int32, (2 * ROWS, 128), 0)
    answers = {}

    def serve(index):
        steps = GROUPS[index]
        for step in steps:
            if step:
                asks[step].wait_recv()
        picks = []
        for pair in (steps[:2], steps[2:]):
            want = jnp.where(lanes < 64, asked[pair[0]], asked[pair[1]])
            picks.append(jnp.where(items == want, 1.0, 0.0).astype(BF16))
        found = lax.dot_general(
            jnp.concatenate(picks, axis=1),
            table[...].reshape(2 * ROWS, D),
            (((0,), (0,)), ((), ())),
            preferred_element_type=F32,
        )
        piece = lax.broadcasted_iota(jnp.int32, (256, 128), 0) & (PIECES - 1)
        packed = jnp.zeros((256, 128), F32)
        for j in range(PIECES):
            packed = jnp.where(piece == j, found[:, j * 128 : (j + 1) * 128], packed)
        served[index] = packed.astype(BF16)
        for place, step in enumerate(steps):
            if step:
                answers[PLANES - step] = send(
                    served.at[index, pl.ds(place * 64, MESSAGE)],
                    rows.at[PLANES - step],
                    at_z(step),
                )
            else:
                rows[0] = packed[place * 64 : place * 64 + MESSAGE].astype(BF16)

    for index in range(len(GROUPS)):
        serve(index)

    relay_q = [weight_relay(wq, half, outer_q[half]) for half in range(2)]
    for half in range(2):
        for copy in inner_r[half]:
            copy.wait_recv()
    outer_r = [weight_outer(wr, half) for half in range(2)]

    def weight_finish(buffer, half, first_hop, relayed, shared):
        first_hop["high_up"].wait_recv()
        shared.append(share(group(buffer, half, 3, 0, SIDE)))
        first_hop["low_down"].wait_recv()
        shared.append(share(group(buffer, half, 1, 0, SIDE)))
        for copy in relayed:
            copy.wait_recv()
        shared.append(share(group(buffer, half, 2, 0, SIDE)))

    for half in range(2):
        weight_finish(wq, half, outer_q[half], relay_q[half], shared_q)
    for half in range(2):
        shared_r += [share(block(wr, half, 0, inner)) for inner in range(1, SIDE)]

    for step in range(1, PLANES):
        answers[step].wait_recv()
    place = chip_col * MESSAGE + rank * PIECES
    column = lax.broadcasted_iota(jnp.int32, (CAND, PLANES * MESSAGE), 1)
    picks = jnp.concatenate(
        [jnp.where(column == place + j, 1.0, 0.0).astype(BF16) for j in range(PIECES)], axis=0
    )
    found = jnp.dot(picks, rows[...].reshape(PLANES * MESSAGE, 128), preferred_element_type=F32)
    for j in range(PIECES):
        fetched[:, j * 128 : (j + 1) * 128] = found[j * CAND : (j + 1) * CAND].astype(BF16)
    normed[...] = norm(fetched[...].astype(F32), gain_in_ref[...]).astype(BF16)

    relay_r = [weight_relay(wr, half, outer_r[half]) for half in range(2)]

    for copy in shared_q:
        copy.wait_recv()
    for core in range(2):
        for half in range(2):
            first = (core * 2 + half) * QUARTER
            projected = jnp.dot(
                normed[...], wq[core, half].reshape(D, QUARTER), preferred_element_type=F32
            )
            active = silu(projected + bias_ref[:, D + first : D + first + QUARTER])
            queries[core, 0, 0, :, half * QUARTER : (half + 1) * QUARTER] = active.astype(BF16)

    inner = []
    for half in range(2):
        mine = queries.at[half, 0, 0]
        inner.append(
            [
                send(mine, queries.at[half, 0, SIDE - step], at_axis(axes[half][0], step))
                for step in (2, 1, 3)
            ]
        )
    outer = []
    for half in range(2):
        for copy in inner[half]:
            copy.wait_recv()
        axis = axes[half][1]
        low, high = queries.at[half, 0, pl.ds(0, 2)], queries.at[half, 0, pl.ds(2, 2)]
        outer.append(
            {
                "low_up": send(low, queries.at[half, 3, pl.ds(0, 2)], at_axis(axis, 1)),
                "high_down": send(high, queries.at[half, 1, pl.ds(2, 2)], at_axis(axis, 3)),
                "high_up": send(high, queries.at[half, 3, pl.ds(2, 2)], at_axis(axis, 1)),
                "low_down": send(low, queries.at[half, 1, pl.ds(0, 2)], at_axis(axis, 3)),
            }
        )

    load_keys.wait()
    load_values.wait()

    def attend(half, step, target):
        for head in range(HEADS // 2):
            there = slice(head * HEAD, (head + 1) * HEAD)
            first = half * HALF + head * HEAD
            query = queries[half, step, :, :, there].reshape(SIDE * CAND, HEAD)
            scores = lax.dot_general(
                query,
                keys[:, first : first + HEAD],
                (((1,), (1,)), ((), ())),
                preferred_element_type=F32,
            )
            weights = silu(scores * HEAD**-0.5).astype(BF16)
            total = jnp.dot(weights, values[:, first : first + HEAD], preferred_element_type=F32)
            target[:, :, there] = total.reshape(SIDE, CAND, HEAD).astype(target.dtype)

    for half in range(2):
        attend(half, 0, own.at[half])

    relay = []
    for half in range(2):
        axis = axes[half][1]
        outer[half]["low_up"].wait_recv()
        up = send(queries.at[half, 3, pl.ds(0, 2)], queries.at[half, 2, pl.ds(0, 2)], at_axis(axis, 1))
        outer[half]["high_down"].wait_recv()
        down = send(queries.at[half, 1, pl.ds(2, 2)], queries.at[half, 2, pl.ds(2, 2)], at_axis(axis, 3))
        relay.append((up, down))

    parts = [[], []]

    def attend_and_send(half, step):
        attend(half, step, part_out.at[half, step])
        parts[half].append(
            send(part_out.at[half, step], part_in.at[half, SIDE - step], at_axis(axes[half][1], step))
        )

    for half in range(2):
        outer[half]["high_up"].wait_recv()
        attend_and_send(half, 3)
    for half in range(2):
        outer[half]["low_down"].wait_recv()
        attend_and_send(half, 1)
    for half in range(2):
        for copy in relay[half]:
            copy.wait_recv()
        attend_and_send(half, 2)

    for half in range(2):
        weight_finish(wr, half, outer_r[half], relay_r[half], shared_r)
    for copy in shared_r:
        copy.wait_recv()
    for core in range(2):
        for half in range(2):
            first = (core * 2 + half) * QUARTER
            projected = jnp.dot(
                normed[...],
                wr[core, half, :, :, :, 0:QUARTER].reshape(D, QUARTER),
                preferred_element_type=F32,
            )
            active = silu(projected + bias_ref[:, first : first + QUARTER])
            gates[:, first : first + QUARTER] = active.astype(BF16)

    totals, sums = [], []
    for half in range(2):
        for copy in parts[half]:
            copy.wait_recv()
        summed = []
        for inner_step in range(SIDE):
            total = own[half, inner_step]
            for step in range(1, SIDE):
                total += part_in[half, step, inner_step].astype(F32)
            summed.append(total)
        copies = []
        for step in (2, 1, 3):
            sum_out[half, step] = summed[step].astype(BF16)
            copies.append(
                send(sum_out.at[half, step], sum_in.at[half, SIDE - step], at_axis(axes[half][0], step))
            )
        totals.append(summed[0])
        sums.append(copies)
    attended = []
    for half in range(2):
        for copy in sums[half]:
            copy.wait_recv()
        total = totals[half]
        for step in range(1, SIDE):
            total += sum_in[half, step].astype(F32)
        attended.append(total)

    gated = norm(jnp.concatenate(attended, axis=1), gain_mid_ref[...])
    gated = (gated * gates[...].astype(F32)).astype(BF16)
    live = hist * CAND + lax.broadcasted_iota(jnp.int32, (CAND, QUARTER), 0) < counts_ref[0]
    for core in range(2):
        for half in range(2):
            first = (core * 2 + half) * QUARTER
            mixed = jnp.dot(
                gated,
                wr[core, half, :, :, :, QUARTER : 2 * QUARTER].reshape(D, QUARTER),
                preferred_element_type=F32,
            )
            mixed += fetched[:, first : first + QUARTER].astype(F32)
            out_ref[:, first : first + QUARTER] = jnp.where(live, mixed, 0.0).astype(BF16)

    for copy in started:
        copy.wait_send()


def local(
    item_table,
    cand_owner,
    cand_row,
    counts,
    hist_keys,
    hist_values,
    gain_in,
    w_in,
    bias_in,
    gain_mid,
    w_out,
):
    vmem = pl.BlockSpec(memory_space=pltpu.VMEM)
    anywhere = pl.BlockSpec(memory_space=pl.ANY)
    events = hist_keys.shape[1]
    result = pl.pallas_call(
        kernel,
        out_shape=jax.ShapeDtypeStruct((CAND, D), BF16),
        in_specs=[
            anywhere,
            vmem,
            vmem,
            pl.BlockSpec(memory_space=pltpu.SMEM),
            anywhere,
            anywhere,
            vmem,
            anywhere,
            vmem,
            vmem,
            anywhere,
        ],
        out_specs=vmem,
        scratch_shapes=[
            pltpu.VMEM((2, ROWS, D), BF16),
            pltpu.VMEM((events, D), BF16),
            pltpu.VMEM((events, D), BF16),
            pltpu.VMEM((2, 2, SIDE, SIDE, SHARD, QUARTER), BF16),
            pltpu.VMEM((2, 2, SIDE, SIDE, SHARD, 2 * QUARTER), BF16),
            pltpu.VMEM((PLANES, 1, 128), jnp.int32),
            pltpu.VMEM((PLANES, 1, 128), jnp.int32),
            pltpu.VMEM((len(GROUPS), 256, 128), BF16),
            pltpu.VMEM((PLANES, MESSAGE, 128), BF16),
            pltpu.VMEM((CAND, D), BF16),
            pltpu.VMEM((CAND, D), BF16),
            pltpu.VMEM((CAND, D), BF16),
            pltpu.VMEM((2, SIDE, SIDE, CAND, HALF), BF16),
            pltpu.VMEM((2, SIDE, CAND, HALF), F32),
            pltpu.VMEM((2, SIDE, SIDE, CAND, HALF), BF16),
            pltpu.VMEM((2, SIDE, SIDE, CAND, HALF), BF16),
            pltpu.VMEM((2, SIDE, CAND, HALF), BF16),
            pltpu.VMEM((2, SIDE, CAND, HALF), BF16),
            pltpu.SemaphoreType.DMA((MESSAGES,)),
            pltpu.SemaphoreType.DMA((MESSAGES,)),
            pltpu.SemaphoreType.DMA((16,)),
        ],
        compiler_params=pltpu.CompilerParams(
            collective_id=0, has_side_effects=True, vmem_limit_bytes=63 << 20
        ),
        name="layer",
    )(
        item_table,
        cand_owner.reshape(1, CAND),
        cand_row,
        counts,
        hist_keys[0],
        hist_values[0],
        gain_in.reshape(1, D),
        w_in,
        bias_in.reshape(1, 2 * D),
        gain_mid.reshape(1, D),
        w_out,
    )
    return result[None]


def solution(mesh):
    placed = (
        P("users", None),
        P("users", "hist", None),
        P("users", "hist"),
        P("users"),
        P("users", "hist", None),
        P("users", "hist", None),
        P(),
        P("hist", None),
        P(),
        P(),
        P("hist", None),
    )
    return jax.shard_map(
        local, mesh=mesh, in_specs=placed, out_specs=P("users", "hist", None), check_vma=False
    )
```

time: 327 us -> 68.6 us (0.21)
  waiting for transfers between devices: 246 us -> 0 us
  Pallas kernels: 0 us -> 65.5 us
  blocking collectives: 28.3 us -> 0 us
  matrix products: 25.3 us -> 0 us
  between operations: 13.9 us -> 0.66 us
  other arithmetic: 5.12 us -> 0 us
  starting transfers between devices: 4.56 us -> 0 us
    all_gather x3 -> x0, waiting for transfers between devices: 134 us -> none  [the longest x1 61.2 us: local(): lax.all_gather(w_out, 'hist', axis=0, tiled=True)]
    reduce_scatter x1 -> x0, waiting for transfers between devices: 88.8 us -> none  [local(): lax.psum_scatter(jnp.concatenate(outputs, axis=1), 'hist', scatter_dimens...]
    pallas_call x0 -> x1, Pallas kernels: none -> 65.5 us  [local(): pl.pallas_call(kernel, out_shape=jax.ShapeDtypeStruct((CAND, D), BF16), i...]
    all_to_all x1 -> x0, blocking collectives: 28.3 us -> none  [local(): lax.all_to_all(requests, 'users', split_axis=0, concat_axis=0, tiled=True)]
    dot_general x10 -> x0, matrix products: 25.3 us -> none  [the longest x8 19.3 us: local(): jnp.dot(weights, values_local[:, first:first + head_size], preferred_elem...]
    all_to_all x1 -> x0, waiting for transfers between devices: 21.9 us -> none  [local(): lax.all_to_all(looked, 'users', split_axis=0, concat_axis=0, tiled=True)]
    all_to_all x1 -> x0, starting transfers between devices: 4.43 us -> none  [local(): lax.all_to_all(looked, 'users', split_axis=0, concat_axis=0, tiled=True)]
    reduce_sum x5 -> x0, other arithmetic: 3.47 us -> none  [the longest x2 1.33 us: layer_norm(): spread = jnp.mean(centred * centred, axis=-1, keepdims=True)]
  transfers between devices with their start and end apart: 5 -> 0, of which waited for: 5 -> 0; matrix products, arithmetic and copies ran while one was open for 3% -> 0% of each run, Pallas kernels for 0% -> 0%
where the time goes in v1:
time: 68.6 us; the launch traced here: 67.7 us
  Pallas kernels  65.5 us (95%)
  local copies, waits for them, and re-layouts  1.54 us (2%)
    pallas_call x1, Pallas kernels, local(): pl.pallas_call(kernel, out_shape=jax.ShapeDtypeStruct((CAND, D), BF16), i...  65.5 us
    unnamed x1, local copies, waits for them, and re-layouts  1.54 us

profile of v1, /device:TPU:1, one launch (start us, length us, event | category | flops | bytes accessed | tf_op | source)
XLA Modules:
  0.0 67.7 jit_solution(15637666932367754522)
XLA Ops:
  0.7 65.5 %layer.1 = bf16[48,1024]{1,0:T(8,128)(2,1)} custom-call(bf16[256,1024]{1,0:T(8,128)(2,1)} %table_ref.1, s32[1,48]{1,0:T(1,128)} %bitcast.13, s32[1,48]{1,0:T(1,128)} %row_row_ref.1, s32[1]{0:T(128)S(6)} %copy.13.counts_ref, bf16[512,1024]{1,0:T(8,128)(2,1)} %bitcast.7, bf16[512,1024]{1,0:T(8,128)(2,1)} %bitcast.8, f32[1,1024]{1,0:T(1,128)} %bitcast.11, ...), custom_call_target="tpu_custom_call" | custom-call | tf_op jit(solution)/shard_map/layer/pallas_call | solution.py:451
  66.2 1.5 %copy.14 = bf16[1,48,1024]{2,1,0:T(8,128)(2,1)} copy(bf16[1,48,1024]{2,1,0:T(8,128)(2,1)} %bitcast.9) | data formatting | bytes 196608

commit v2 on v1

v2 whole, which is shorter than its diff:
```python
import functools

import jax
import jax.numpy as jnp
from jax import lax
from jax.experimental import pallas as pl
from jax.experimental.pallas import tpu as pltpu
from jax.sharding import PartitionSpec as P

MESH = pl.DeviceIdType.MESH
F32, BF16 = jnp.float32, jnp.bfloat16

HEADS = 8
HEAD = 128
D = 1024
HALF = D // 2
QUARTER = D // 4
CAND = 48
ROWS = 256
PLANES = 16
SIDE = 4
SHARD = D // (SIDE * SIDE)
SLOTS = 6
PIECES = 8
MESSAGE = SLOTS * PIECES
EPS = 1e-05
RELAYED = ((0, 1), (1, 1), (2, 3), (3, 3))
SEMAPHORES = 81

GROUPS = ((1, 15, 2, 14), (3, 13, 4, 12), (5, 11, 6, 10), (7, 9, 8, 0))


def norm(values, gain):
    mean = jnp.mean(values, axis=-1, keepdims=True)
    centred = values - mean
    spread = jnp.mean(centred * centred, axis=-1, keepdims=True)
    return centred * lax.rsqrt(spread + EPS) * gain


def silu(values, scale=1.0):
    half = values * (0.5 * scale)
    return half + half * jnp.tanh(half)


def kernel(
    table_hbm,
    owner_hbm,
    row_hbm,
    counts_hbm,
    keys_hbm,
    values_hbm,
    gain_in_hbm,
    w_in_ref,
    bias_hbm,
    gain_mid_hbm,
    w_out_ref,
    out_ref,
    owner_row_ref,
    row_row_ref,
    counts_ref,
    gain_in_ref,
    bias_ref,
    gain_mid_ref,
    table,
    keys,
    values,
    wq,
    wr,
    plan,
    asked,
    spread,
    served,
    rows,
    fetched,
    normed,
    gates,
    queries,
    own,
    part_out,
    part_in,
    sum_out,
    sum_in,
    semaphores,
):
    users, hist = lax.axis_index("users"), lax.axis_index("hist")
    z, c = users // 2, lax.rem(users, 2)
    x, y = hist // SIDE, lax.rem(hist, SIDE)

    def at_z(step):
        return (lax.rem(z + step, PLANES) * 2 + c, hist)

    def at_axis(axis, step):
        if axis == "x":
            return (users, lax.rem(x + step, SIDE) * SIDE + y)
        return (users, x * SIDE + lax.rem(y + step, SIDE))

    partner = (z * 2 + 1 - c, hist)
    used, unsent = [], []

    def new():
        used.append(0)
        return semaphores.at[len(used) - 1]

    def send(src, dst, device, sent, landed):
        pltpu.make_async_remote_copy(
            src_ref=src,
            dst_ref=dst,
            send_sem=sent,
            recv_sem=landed,
            device_id=device,
            device_id_type=MESH,
        ).start()

    def wait(semaphore, like):
        pltpu.make_async_copy(like, like, semaphore).wait()

    def sending(like):
        semaphore = new()
        unsent.append((semaphore, like))
        return semaphore

    barrier = pltpu.get_barrier_semaphore()
    peers = [at_z(step) for step in range(1, PLANES)] + [partner]
    peers += [at_axis(axis, step) for axis in "xy" for step in range(1, SIDE)]
    for peer in peers:
        pl.semaphore_signal(barrier, inc=1, device_id=peer, device_id_type=MESH)

    def load(src, dst):
        copy = pltpu.make_async_copy(src, dst, new())
        copy.start()
        return copy

    load_small = [load(owner_hbm, owner_row_ref), load(row_hbm, row_row_ref)]
    load_weights = new()
    for core in range(2):
        for half in range(2):
            first = (core * 2 + half) * QUARTER
            mine = wr.at[core, half, x, y]
            for src, dst in (
                (w_in_ref.at[:, pl.ds(D + first, QUARTER)], wq.at[core, half, x, y]),
                (w_in_ref.at[:, pl.ds(first, QUARTER)], mine.at[:, pl.ds(0, QUARTER)]),
                (w_out_ref.at[:, pl.ds(first, QUARTER)], mine.at[:, pl.ds(QUARTER, QUARTER)]),
            ):
                pltpu.make_async_copy(src, dst, load_weights).start()
    load_table = load(table_hbm, table.at[c])
    load_late = [
        load(gain_in_hbm, gain_in_ref),
        load(bias_hbm, bias_ref),
        load(gain_mid_hbm, gain_mid_ref),
        load(counts_hbm, counts_ref),
        load(keys_hbm, keys),
        load(values_hbm, values),
    ]

    for copy in load_small:
        copy.wait()

    chip_row = ((owner_row_ref[...] >> 1) - z) & (PLANES - 1)
    later = lax.broadcasted_iota(jnp.int32, (CAND, CAND), 0)
    earlier = lax.broadcasted_iota(jnp.int32, (CAND, CAND), 1)
    chip_col = jnp.where(earlier == later, chip_row.astype(F32), 0.0)
    chip_col = jnp.sum(chip_col, axis=1, keepdims=True).astype(jnp.int32)
    before = earlier < later
    same = jnp.where((chip_col == chip_row) & before, 1.0, 0.0)
    rank = jnp.sum(same, axis=1, keepdims=True).astype(jnp.int32)
    lane = lax.broadcasted_iota(jnp.int32, (CAND, 128), 1) & 7
    slot_of = jnp.where(lane == rank, 1.0, 0.0).astype(BF16)
    chip_of = chip_row == lax.broadcasted_iota(jnp.int32, (PLANES, CAND), 0)
    row_part = jnp.where(chip_of, row_row_ref[...].astype(F32), 0.0).astype(BF16)
    core_part = jnp.where(chip_of, ((owner_row_ref[...] & 1) + 1).astype(F32), 0.0).astype(BF16)
    wanted = jnp.dot(row_part, slot_of, preferred_element_type=F32)
    wanted += (jnp.dot(core_part, slot_of, preferred_element_type=F32) - 1.0) * ROWS
    wanted = wanted.astype(jnp.int32)
    for step in range(PLANES):
        plan[step] = wanted[step : step + 1]
    asked[0] = wanted[0:1]

    wait(load_weights, wq.at[0, 0, pl.ds(0, 3)])
    pl.semaphore_wait(barrier, len(peers))

    table_landed = new()
    send(table_hbm, table.at[c], partner, sending(table_hbm), table_landed)
    ask_sent = sending(plan.at[pl.ds(1, PLANES - 1)])
    ask_landed = [new() for _ in GROUPS]
    for step in (8, 7, 9, 6, 10, 5, 11, 4, 12, 3, 13, 2, 14, 1, 15):
        (index,) = [i for i, steps in enumerate(GROUPS) if PLANES - step in steps]
        send(plan.at[step], asked.at[PLANES - step], at_z(step), ask_sent, ask_landed[index])

    axes = (("y", "x"), ("x", "y"))

    def block(buffer, half, outer, inner):
        if half == 0:
            return buffer.at[c, 0, lax.rem(x + outer, SIDE), lax.rem(y + inner, SIDE)]
        return buffer.at[c, 1, lax.rem(x + inner, SIDE), lax.rem(y + outer, SIDE)]

    def group(buffer, half, outer, first, count):
        if half == 0:
            return buffer.at[c, 0, lax.rem(x + outer, SIDE), pl.ds(first, count)]
        return buffer.at[c, 1, pl.ds(first, count), lax.rem(y + outer, SIDE)]

    def several(buffer, outer):
        return buffer.at[0, :, pl.ds(0, 3)] if outer else buffer.at[0, :, 0, pl.ds(0, 3)]

    class Gather:
        def __init__(self, buffer):
            self.buffer = buffer
            self.two, self.four = buffer.at[0, 0, 0, pl.ds(0, 2)], buffer.at[0, 0, 0]
            self.inner_sent, self.outer_sent = sending(several(buffer, 0)), sending(several(buffer, 1))
            self.share_sent = [sending(several(buffer, 0)), sending(several(buffer, 1))]
            self.share_landed = [new(), new()]
            self.inner_landed = new()
            self.landed = [[new() for _ in range(5)] for _ in range(2)]

        def inner(self):
            for half in range(2):
                mine = block(self.buffer, half, 0, 0)
                for step in (2, 1, 3):
                    send(mine, mine, at_axis(axes[half][0], step), self.inner_sent, self.inner_landed)

        def outer(self):
            wait(self.inner_landed, several(self.buffer, 0))
            for half in range(2):
                for index, (first, step) in enumerate(((0, 1), (2, 3), (2, 1), (0, 3))):
                    part = group(self.buffer, half, 0, first, 2)
                    device = at_axis(axes[half][1], step)
                    send(part, part, device, self.outer_sent, self.landed[half][index])

        def share_inner(self):
            for half in range(2):
                for step in range(1, SIDE):
                    part = block(self.buffer, half, 0, step)
                    send(part, part, partner, self.share_sent[0], self.share_landed[0])

        def relay(self):
            for half in range(2):
                for index, (first, step) in enumerate(((0, 1), (2, 3))):
                    wait(self.landed[half][index], self.two)
                    part = group(self.buffer, half, SIDE - step, first, 2)
                    device = at_axis(axes[half][1], step)
                    send(part, part, device, self.outer_sent, self.landed[half][4])

        def finish(self):
            for half in range(2):
                for index, outer, like in ((2, 3, self.two), (3, 1, self.two), (4, 2, self.four)):
                    wait(self.landed[half][index], like)
                    part = group(self.buffer, half, outer, 0, SIDE)
                    send(part, part, partner, self.share_sent[1], self.share_landed[1])

        def ready(self):
            wait(self.share_landed[0], several(self.buffer, 0))
            wait(self.share_landed[1], several(self.buffer, 1))

    gather_q, gather_r = Gather(wq), Gather(wr)
    gather_q.inner()

    load_table.wait()
    wait(table_landed, table.at[0])
    lanes = lax.broadcasted_iota(jnp.int32, (1, 128), 1)
    items = lax.broadcasted_iota(jnp.int32, (2 * ROWS, 128), 0)
    answer_sent, answer_landed = sending(rows.at[pl.ds(1, PLANES - 1)]), new()

    def serve(index):
        steps = GROUPS[index]
        wait(ask_landed[index], asked.at[pl.ds(1, len([step for step in steps if step]))])
        want = asked[steps[0]]
        for place in range(1, SIDE):
            want = jnp.where(lanes >> 3 == place, asked[steps[place]], want)
        picks = jnp.where((items == want) & (lanes < 32), 1.0, 0.0).astype(BF16)
        found = lax.dot_general(
            picks, table[...].reshape(2 * ROWS, D), (((0,), (0,)), ((), ())), preferred_element_type=F32
        )
        for j in range(PIECES):
            spread[pl.ds(j, 32, stride=PIECES), :] = found[:32, j * 128 : (j + 1) * 128]
        served[index] = spread[...].astype(BF16)
        for place, step in enumerate(steps):
            if step:
                send(
                    served.at[index, pl.ds(place * 64, MESSAGE)],
                    rows.at[PLANES - step],
                    at_z(step),
                    answer_sent,
                    answer_landed,
                )
            else:
                rows[0] = served[index, place * 64 : place * 64 + MESSAGE]

    for index in range(len(GROUPS)):
        serve(index)
    gather_q.outer()
    gather_r.inner()
    gather_q.share_inner()
    gather_q.relay()
    gather_r.outer()
    gather_q.finish()
    gather_r.share_inner()

    wait(answer_landed, rows.at[pl.ds(1, PLANES - 1)])
    place = chip_col * MESSAGE + rank * PIECES
    column = lax.broadcasted_iota(jnp.int32, (CAND, PLANES * MESSAGE), 1)
    picks = jnp.concatenate(
        [jnp.where(column == place + j, 1.0, 0.0).astype(BF16) for j in range(PIECES)], axis=0
    )
    found = jnp.dot(picks, rows[...].reshape(PLANES * MESSAGE, 128), preferred_element_type=F32)
    for j in range(PIECES):
        fetched[:, j * 128 : (j + 1) * 128] = found[j * CAND : (j + 1) * CAND].astype(BF16)
    for copy in load_late:
        copy.wait()
    normed[...] = norm(fetched[...].astype(F32), gain_in_ref[...]).astype(BF16)

    gather_r.relay()
    gather_q.ready()
    for core in range(2):
        for half in range(2):
            first = (core * 2 + half) * QUARTER
            projected = jnp.dot(
                normed[...], wq[core, half].reshape(D, QUARTER), preferred_element_type=F32
            )
            active = silu(projected + bias_ref[:, D + first : D + first + QUARTER])
            queries[core, 0, 0, :, half * QUARTER : (half + 1) * QUARTER] = active.astype(BF16)

    query_sent = [sending(queries.at[:, 0, pl.ds(0, 3)]), sending(queries.at[:, pl.ds(0, 3)])]
    inner_landed = [{step: new() for step in (2, 1, 3)} for _ in range(2)]
    for half in range(2):
        mine = queries.at[half, 0, 0]
        for step in (2, 1, 3):
            send(
                mine,
                queries.at[half, 0, SIDE - step],
                at_axis(axes[half][0], step),
                query_sent[0],
                inner_landed[half][step],
            )
    outer_landed = []
    for half in range(2):
        landed = {step: new() for step in (1, 2, 3)}
        outer_landed.append((landed, {key: new() for key in RELAYED}))

    def send_block(half, place):
        for step in (1, 3):
            together, alone = outer_landed[half]
            send(
                queries.at[half, 0, place],
                queries.at[half, SIDE - step, place],
                at_axis(axes[half][1], step),
                query_sent[1],
                alone[place, step] if (place, step) in RELAYED else together[step],
            )

    def relay_block(half, place, step):
        together, alone = outer_landed[half]
        wait(alone[place, step], queries.at[half, 0, 0])
        send(
            queries.at[half, SIDE - step, place],
            queries.at[half, 2, place],
            at_axis(axes[half][1], step),
            query_sent[1],
            together[2],
        )

    for half in range(2):
        send_block(half, 0)
    for step, place in ((1, 3), (3, 1), (2, 2)):
        for half in range(2):
            wait(inner_landed[half][step], queries.at[half, 0, 0])
            send_block(half, place)

    def attend(half, step, target):
        scores = []
        for head in range(HEADS // 2):
            there = slice(head * HEAD, (head + 1) * HEAD)
            first = half * HALF + head * HEAD
            query = queries[half, step, :, :, there].reshape(SIDE * CAND, HEAD)
            scores.append(
                lax.dot_general(
                    query,
                    keys[:, first : first + HEAD],
                    (((1,), (1,)), ((), ())),
                    preferred_element_type=F32,
                )
            )
        for head in range(HEADS // 2):
            there = slice(head * HEAD, (head + 1) * HEAD)
            first = half * HALF + head * HEAD
            weights = silu(scores[head], HEAD**-0.5).astype(BF16)
            total = jnp.dot(weights, values[:, first : first + HEAD], preferred_element_type=F32)
            target[:, :, there] = total.reshape(SIDE, CAND, HEAD).astype(target.dtype)

    for half in range(2):
        attend(half, 0, own.at[half])

    for place, step in ((0, 1), (3, 3), (1, 1), (2, 3)):
        for half in range(2):
            relay_block(half, place, step)

    part_sent = sending(part_out.at[:, pl.ds(1, 3)])
    part_landed = [new() for _ in range(2)]

    def attend_and_send(half, step):
        attend(half, step, part_out.at[half, step])
        send(
            part_out.at[half, step],
            part_in.at[half, SIDE - step],
            at_axis(axes[half][1], step),
            part_sent,
            part_landed[half],
        )

    for step in (3, 1, 2):
        for half in range(2):
            count = 4 if step == 2 else 2
            wait(outer_landed[half][0][SIDE - step], queries.at[half, 0, pl.ds(0, count)])
            attend_and_send(half, step)

    gather_r.finish()
    gather_r.ready()
    for core in range(2):
        for half in range(2):
            first = (core * 2 + half) * QUARTER
            projected = jnp.dot(
                normed[...],
                wr[core, half, :, :, :, 0:QUARTER].reshape(D, QUARTER),
                preferred_element_type=F32,
            )
            active = silu(projected + bias_ref[:, first : first + QUARTER])
            gates[:, first : first + QUARTER] = active.astype(BF16)

    totals = []
    sum_sent = sending(sum_out.at[:, pl.ds(1, 3)])
    sum_landed = [new() for _ in range(2)]
    for half in range(2):
        wait(part_landed[half], part_in.at[half, pl.ds(1, 3)])
        summed = []
        for inner_step in range(SIDE):
            total = own[half, inner_step]
            for step in range(1, SIDE):
                total += part_in[half, step, inner_step].astype(F32)
            summed.append(total)
        for step in (2, 1, 3):
            sum_out[half, step] = summed[step].astype(BF16)
            send(
                sum_out.at[half, step],
                sum_in.at[half, SIDE - step],
                at_axis(axes[half][0], step),
                sum_sent,
                sum_landed[half],
            )
        totals.append(summed[0])
    attended = []
    for half in range(2):
        wait(sum_landed[half], sum_in.at[half, pl.ds(1, 3)])
        total = totals[half]
        for step in range(1, SIDE):
            total += sum_in[half, step].astype(F32)
        attended.append(total)

    gated = norm(jnp.concatenate(attended, axis=1), gain_mid_ref[...])
    gated = (gated * gates[...].astype(F32)).astype(BF16)
    live = hist * CAND + lax.broadcasted_iota(jnp.int32, (CAND, QUARTER), 0) < counts_ref[...]
    for core in range(2):
        for half in range(2):
            first = (core * 2 + half) * QUARTER
            mixed = jnp.dot(
                gated,
                wr[core, half, :, :, :, QUARTER : 2 * QUARTER].reshape(D, QUARTER),
                preferred_element_type=F32,
            )
            mixed += fetched[:, first : first + QUARTER].astype(F32)
            out_ref[:, first : first + QUARTER] = jnp.where(live, mixed, 0.0).astype(BF16)

    for semaphore, like in unsent:
        wait(semaphore, like)
    assert len(used) == SEMAPHORES, len(used)


def local(
    item_table,
    cand_owner,
    cand_row,
    counts,
    hist_keys,
    hist_values,
    gain_in,
    w_in,
    bias_in,
    gain_mid,
    w_out,
):
    vmem = pl.BlockSpec(memory_space=pltpu.VMEM)
    anywhere = pl.BlockSpec(memory_space=pl.ANY)
    events = hist_keys.shape[1]
    result = pl.pallas_call(
        kernel,
        out_shape=jax.ShapeDtypeStruct((CAND, D), BF16),
        in_specs=[anywhere] * 11,
        out_specs=vmem,
        scratch_shapes=[
            pltpu.VMEM((1, CAND), jnp.int32),
            pltpu.VMEM((1, CAND), jnp.int32),
            pltpu.VMEM((1, 1), jnp.int32),
            pltpu.VMEM((1, D), F32),
            pltpu.VMEM((1, 2 * D), F32),
            pltpu.VMEM((1, D), F32),
            pltpu.VMEM((2, ROWS, D), BF16),
            pltpu.VMEM((events, D), BF16),
            pltpu.VMEM((events, D), BF16),
            pltpu.VMEM((2, 2, SIDE, SIDE, SHARD, QUARTER), BF16),
            pltpu.VMEM((2, 2, SIDE, SIDE, SHARD, 2 * QUARTER), BF16),
            pltpu.VMEM((PLANES, 1, 128), jnp.int32),
            pltpu.VMEM((PLANES, 1, 128), jnp.int32),
            pltpu.VMEM((256, 128), F32),
            pltpu.VMEM((len(GROUPS), 256, 128), BF16),
            pltpu.VMEM((PLANES, MESSAGE, 128), BF16),
            pltpu.VMEM((CAND, D), BF16),
            pltpu.VMEM((CAND, D), BF16),
            pltpu.VMEM((CAND, D), BF16),
            pltpu.VMEM((2, SIDE, SIDE, CAND, HALF), BF16),
            pltpu.VMEM((2, SIDE, CAND, HALF), F32),
            pltpu.VMEM((2, SIDE, SIDE, CAND, HALF), BF16),
            pltpu.VMEM((2, SIDE, SIDE, CAND, HALF), BF16),
            pltpu.VMEM((2, SIDE, CAND, HALF), BF16),
            pltpu.VMEM((2, SIDE, CAND, HALF), BF16),
            pltpu.SemaphoreType.DMA((SEMAPHORES,)),
        ],
        compiler_params=pltpu.CompilerParams(
            collective_id=0, has_side_effects=True, vmem_limit_bytes=63 << 20
        ),
        name="layer",
    )(
        item_table,
        cand_owner.reshape(1, CAND),
        cand_row,
        counts.reshape(1, 1),
        hist_keys[0],
        hist_values[0],
        gain_in.reshape(1, D),
        w_in,
        bias_in.reshape(1, 2 * D),
        gain_mid.reshape(1, D),
        w_out,
    )
    return result[None]


def solution(mesh):
    placed = (
        P("users", None),
        P("users", "hist", None),
        P("users", "hist"),
        P("users"),
        P("users", "hist", None),
        P("users", "hist", None),
        P(),
        P("hist", None),
        P(),
        P(),
        P("hist", None),
    )
    return jax.shard_map(
        local, mesh=mesh, in_specs=placed, out_specs=P("users", "hist", None), check_vma=False
    )
```

time: 68.6 us -> 66.8 us (0.974)
  the two profiles are of different devices: /device:TPU:1 before, /device:TPU:32 now
where the time goes in v2:
time: 66.8 us; the launch traced here: 66.7 us
  Pallas kernels  64.5 us (97%)
  local copies, waits for them, and re-layouts  1.54 us (2%)
    pallas_call x1, Pallas kernels, local(): pl.pallas_call(kernel, out_shape=jax.ShapeDtypeStruct((CAND, D), BF16), i...  64.5 us
    unnamed x1, local copies, waits for them, and re-layouts  1.54 us

profile of v2, /device:TPU:32, one launch (start us, length us, event | category | flops | bytes accessed | tf_op | source)
XLA Modules:
  0.0 66.7 jit_solution(14797279011838432474)
XLA Ops:
  0.7 64.5 %layer.1 = bf16[48,1024]{1,0:T(8,128)(2,1)} custom-call(bf16[256,1024]{1,0:T(8,128)(2,1)} %table_hbm.1, s32[1,48]{1,0:T(1,128)} %bitcast.15, s32[1,48]{1,0:T(1,128)} %row_hbm.1, s32[1,1]{1,0:T(1,128)} %bitcast.8.counts_hbm, bf16[512,1024]{1,0:T(8,128)(2,1)} %bitcast.9, bf16[512,1024]{1,0:T(8,128)(2,1)} %bitcast.10, f32[1,1024]{1,0:T(1,128)} %bitcast.13, ...), custom_call_target="tpu_custom_call" | custom-call | tf_op jit(solution)/shard_map/layer/pallas_call | solution.py:491
  65.1 1.5 %copy.14 = bf16[1,48,1024]{2,1,0:T(8,128)(2,1)} copy(bf16[1,48,1024]{2,1,0:T(8,128)(2,1)} %bitcast.11) | data formatting | bytes 196608

commit v3 on v2

--- a/solution.py
+++ b/solution.py
@@ -24,7 +24,7 @@
 PIECES = 8
 MESSAGE = SLOTS * PIECES
 EPS = 1e-05
-RELAYED = ((0, 1), (1, 1), (2, 3), (3, 3))
+RELAYED = ((0, 1), (1, 1), (3, 3))
 SEMAPHORES = 81
 
 GROUPS = ((1, 15, 2, 14), (3, 13, 4, 12), (5, 11, 6, 10), (7, 9, 8, 0))
@@ -284,9 +284,11 @@
             else:
                 rows[0] = served[index, place * 64 : place * 64 + MESSAGE]
 
-    for index in range(len(GROUPS)):
-        serve(index)
+    serve(0)
+    serve(1)
     gather_q.outer()
+    serve(2)
+    serve(3)
     gather_r.inner()
     gather_q.share_inner()
     gather_q.relay()
@@ -309,41 +311,24 @@
 
     gather_r.relay()
     gather_q.ready()
-    for core in range(2):
-        for half in range(2):
-            first = (core * 2 + half) * QUARTER
-            projected = jnp.dot(
-                normed[...], wq[core, half].reshape(D, QUARTER), preferred_element_type=F32
-            )
-            active = silu(projected + bias_ref[:, D + first : D + first + QUARTER])
-            queries[core, 0, 0, :, half * QUARTER : (half + 1) * QUARTER] = active.astype(BF16)
 
     query_sent = [sending(queries.at[:, 0, pl.ds(0, 3)]), sending(queries.at[:, pl.ds(0, 3)])]
     inner_landed = [{step: new() for step in (2, 1, 3)} for _ in range(2)]
-    for half in range(2):
-        mine = queries.at[half, 0, 0]
-        for step in (2, 1, 3):
-            send(
-                mine,
-                queries.at[half, 0, SIDE - step],
-                at_axis(axes[half][0], step),
-                query_sent[0],
-                inner_landed[half][step],
-            )
     outer_landed = []
     for half in range(2):
-        landed = {step: new() for step in (1, 2, 3)}
+        landed = {key: new() for key in (1, 3, "low", "high")}
         outer_landed.append((landed, {key: new() for key in RELAYED}))
 
     def send_block(half, place):
-        for step in (1, 3):
-            together, alone = outer_landed[half]
+        together, alone = outer_landed[half]
+        for step in (2, 1, 3) if place == 2 else (1, 3):
+            landed = together["high" if step == 2 else step]
             send(
                 queries.at[half, 0, place],
                 queries.at[half, SIDE - step, place],
                 at_axis(axes[half][1], step),
                 query_sent[1],
-                alone[place, step] if (place, step) in RELAYED else together[step],
+                alone[place, step] if (place, step) in RELAYED else landed,
             )
 
     def relay_block(half, place, step):
@@ -354,22 +339,38 @@
             queries.at[half, 2, place],
             at_axis(axes[half][1], step),
             query_sent[1],
-            together[2],
+            together["low" if place < 2 else "high"],
         )
 
     for half in range(2):
+        for piece in range(2):
+            first = D + half * HALF + piece * QUARTER
+            projected = jnp.dot(
+                normed[...], wq[half, piece].reshape(D, QUARTER), preferred_element_type=F32
+            )
+            active = silu(projected + bias_ref[:, first : first + QUARTER])
+            queries[half, 0, 0, :, piece * QUARTER : (piece + 1) * QUARTER] = active.astype(BF16)
+        for step in (2, 1, 3):
+            send(
+                queries.at[half, 0, 0],
+                queries.at[half, 0, SIDE - step],
+                at_axis(axes[half][0], step),
+                query_sent[0],
+                inner_landed[half][step],
+            )
         send_block(half, 0)
     for step, place in ((1, 3), (3, 1), (2, 2)):
         for half in range(2):
             wait(inner_landed[half][step], queries.at[half, 0, 0])
             send_block(half, place)
 
-    def attend(half, step, target):
+    def attend(half, step, target, first_block=0, count=SIDE):
+        blocks = slice(first_block, first_block + count)
         scores = []
         for head in range(HEADS // 2):
             there = slice(head * HEAD, (head + 1) * HEAD)
             first = half * HALF + head * HEAD
-            query = queries[half, step, :, :, there].reshape(SIDE * CAND, HEAD)
+            query = queries[half, step, blocks, :, there].reshape(count * CAND, HEAD)
             scores.append(
                 lax.dot_general(
                     query,
@@ -383,33 +384,38 @@
             first = half * HALF + head * HEAD
             weights = silu(scores[head], HEAD**-0.5).astype(BF16)
             total = jnp.dot(weights, values[:, first : first + HEAD], preferred_element_type=F32)
-            target[:, :, there] = total.reshape(SIDE, CAND, HEAD).astype(target.dtype)
+            target[blocks, :, there] = total.reshape(count, CAND, HEAD).astype(target.dtype)
 
     for half in range(2):
         attend(half, 0, own.at[half])
 
-    for place, step in ((0, 1), (3, 3), (1, 1), (2, 3)):
+    for place, step in ((0, 1), (3, 3), (1, 1)):
         for half in range(2):
             relay_block(half, place, step)
 
     part_sent = sending(part_out.at[:, pl.ds(1, 3)])
     part_landed = [new() for _ in range(2)]
 
-    def attend_and_send(half, step):
-        attend(half, step, part_out.at[half, step])
+    def attend_and_send(half, step, first, count):
+        attend(half, step, part_out.at[half, step], first, count)
+        blocks = pl.ds(first, count)
         send(
-            part_out.at[half, step],
-            part_in.at[half, SIDE - step],
+            part_out.at[half, step, blocks],
+            part_in.at[half, SIDE - step, blocks],
             at_axis(axes[half][1], step),
             part_sent,
             part_landed[half],
         )
 
-    for step in (3, 1, 2):
+    for step, first, count, key, landed in (
+        (3, 0, SIDE, 1, 2),
+        (1, 0, SIDE, 3, 3),
+        (2, 0, 2, "low", 2),
+        (2, 2, 2, "high", 2),
+    ):
         for half in range(2):
-            count = 4 if step == 2 else 2
-            wait(outer_landed[half][0][SIDE - step], queries.at[half, 0, pl.ds(0, count)])
-            attend_and_send(half, step)
+            wait(outer_landed[half][0][key], queries.at[half, 0, pl.ds(0, landed)])
+            attend_and_send(half, step, first, count)
 
     gather_r.finish()
     gather_r.ready()
@@ -429,14 +435,15 @@
     sum_landed = [new() for _ in range(2)]
     for half in range(2):
         wait(part_landed[half], part_in.at[half, pl.ds(1, 3)])
-        summed = []
-        for inner_step in range(SIDE):
-            total = own[half, inner_step]
+
+        def summed(place):
+            total = own[half, place]
             for step in range(1, SIDE):
-                total += part_in[half, step, inner_step].astype(F32)
-            summed.append(total)
+                total += part_in[half, step, place].astype(F32)
+            return total
+
         for step in (2, 1, 3):
-            sum_out[half, step] = summed[step].astype(BF16)
+            sum_out[half, step] = summed(step).astype(BF16)
             send(
                 sum_out.at[half, step],
                 sum_in.at[half, SIDE - step],
@@ -444,7 +451,7 @@
                 sum_sent,
                 sum_landed[half],
             )
-        totals.append(summed[0])
+        totals.append(summed(0))
     attended = []
     for half in range(2):
         wait(sum_landed[half], sum_in.at[half, pl.ds(1, 3)])

time: 66.8 us -> 66 us (0.988)
  the two profiles are of different devices: /device:TPU:32 before, /device:TPU:1 now
where the time goes in v3:
time: 66 us; the launch traced here: 65.4 us
  Pallas kernels  63.2 us (96%)
  local copies, waits for them, and re-layouts  1.54 us (2%)
  between operations  0.66 us (1%)
    pallas_call x1, Pallas kernels, local(): pl.pallas_call(kernel, out_shape=jax.ShapeDtypeStruct((CAND, D), BF16), i...  63.2 us
    unnamed x1, local copies, waits for them, and re-layouts  1.54 us

profile of v3, /device:TPU:1, one launch (start us, length us, event | category | flops | bytes accessed | tf_op | source)
XLA Modules:
  0.0 65.4 jit_solution(13328833975088743353)
XLA Ops:
  0.7 63.2 %layer.1 = bf16[48,1024]{1,0:T(8,128)(2,1)} custom-call(bf16[256,1024]{1,0:T(8,128)(2,1)} %table_hbm.1, s32[1,48]{1,0:T(1,128)} %bitcast.15, s32[1,48]{1,0:T(1,128)} %row_hbm.1, s32[1,1]{1,0:T(1,128)} %bitcast.8.counts_hbm, bf16[512,1024]{1,0:T(8,128)(2,1)} %bitcast.9, bf16[512,1024]{1,0:T(8,128)(2,1)} %bitcast.10, f32[1,1024]{1,0:T(1,128)} %bitcast.13, ...), custom_call_target="tpu_custom_call" | custom-call | tf_op jit(solution)/shard_map/layer/pallas_call | solution.py:498
  63.9 1.5 %copy.14 = bf16[1,48,1024]{2,1,0:T(8,128)(2,1)} copy(bf16[1,48,1024]{2,1,0:T(8,128)(2,1)} %bitcast.11) | data formatting | bytes 196608

commit v4 on v3

--- a/solution.py
+++ b/solution.py
@@ -25,7 +25,7 @@
 MESSAGE = SLOTS * PIECES
 EPS = 1e-05
 RELAYED = ((0, 1), (1, 1), (3, 3))
-SEMAPHORES = 81
+SEMAPHORES = 85
 
 GROUPS = ((1, 15, 2, 14), (3, 13, 4, 12), (5, 11, 6, 10), (7, 9, 8, 0))
 
@@ -54,6 +54,7 @@
     bias_hbm,
     gain_mid_hbm,
     w_out_ref,
+    out_hbm,
     out_ref,
     owner_row_ref,
     row_row_ref,
@@ -68,6 +69,7 @@
     wr,
     plan,
     asked,
+    order,
     spread,
     served,
     rows,
@@ -120,7 +122,8 @@
         return semaphore
 
     barrier = pltpu.get_barrier_semaphore()
-    peers = [at_z(step) for step in range(1, PLANES)] + [partner]
+    far_first = (8, 7, 9, 6, 10, 5, 11, 4, 12, 3, 13, 2, 14, 1, 15)
+    peers = [at_z(step) for step in far_first] + [partner]
     peers += [at_axis(axis, step) for axis in "xy" for step in range(1, SIDE)]
     for peer in peers:
         pl.semaphore_signal(barrier, inc=1, device_id=peer, device_id_type=MESH)
@@ -175,6 +178,12 @@
         plan[step] = wanted[step : step + 1]
     asked[0] = wanted[0:1]
 
+    place = chip_col * MESSAGE + rank * PIECES
+    column = lax.broadcasted_iota(jnp.int32, (CAND, PLANES * MESSAGE), 1)
+    for j in range(PIECES):
+        picked = jnp.where(column == place + j, 1.0, 0.0).astype(BF16)
+        order[j * CAND : (j + 1) * CAND] = picked
+
     wait(load_weights, wq.at[0, 0, pl.ds(0, 3)])
     pl.semaphore_wait(barrier, len(peers))
 
@@ -182,7 +191,7 @@
     send(table_hbm, table.at[c], partner, sending(table_hbm), table_landed)
     ask_sent = sending(plan.at[pl.ds(1, PLANES - 1)])
     ask_landed = [new() for _ in GROUPS]
-    for step in (8, 7, 9, 6, 10, 5, 11, 4, 12, 3, 13, 2, 14, 1, 15):
+    for step in far_first:
         (index,) = [i for i, steps in enumerate(GROUPS) if PLANES - step in steps]
         send(plan.at[step], asked.at[PLANES - step], at_z(step), ask_sent, ask_landed[index])
 
@@ -297,12 +306,7 @@
     gather_r.share_inner()
 
     wait(answer_landed, rows.at[pl.ds(1, PLANES - 1)])
-    place = chip_col * MESSAGE + rank * PIECES
-    column = lax.broadcasted_iota(jnp.int32, (CAND, PLANES * MESSAGE), 1)
-    picks = jnp.concatenate(
-        [jnp.where(column == place + j, 1.0, 0.0).astype(BF16) for j in range(PIECES)], axis=0
-    )
-    found = jnp.dot(picks, rows[...].reshape(PLANES * MESSAGE, 128), preferred_element_type=F32)
+    found = jnp.dot(order[...], rows[...].reshape(PLANES * MESSAGE, 128), preferred_element_type=F32)
     for j in range(PIECES):
         fetched[:, j * 128 : (j + 1) * 128] = found[j * CAND : (j + 1) * CAND].astype(BF16)
     for copy in load_late:
@@ -462,6 +466,7 @@
 
     gated = norm(jnp.concatenate(attended, axis=1), gain_mid_ref[...])
     gated = (gated * gates[...].astype(F32)).astype(BF16)
+    stores = []
     live = hist * CAND + lax.broadcasted_iota(jnp.int32, (CAND, QUARTER), 0) < counts_ref[...]
     for core in range(2):
         for half in range(2):
@@ -472,10 +477,14 @@
                 preferred_element_type=F32,
             )
             mixed += fetched[:, first : first + QUARTER].astype(F32)
-            out_ref[:, first : first + QUARTER] = jnp.where(live, mixed, 0.0).astype(BF16)
+            there = pl.ds(first, QUARTER)
+            out_ref[:, there] = jnp.where(live, mixed, 0.0).astype(BF16)
+            stores.append(load(out_ref.at[:, there], out_hbm.at[:, there]))
 
     for semaphore, like in unsent:
         wait(semaphore, like)
+    for copy in stores:
+        copy.wait()
     assert len(used) == SEMAPHORES, len(used)
 
 
@@ -492,15 +501,15 @@
     gain_mid,
     w_out,
 ):
-    vmem = pl.BlockSpec(memory_space=pltpu.VMEM)
     anywhere = pl.BlockSpec(memory_space=pl.ANY)
     events = hist_keys.shape[1]
     result = pl.pallas_call(
         kernel,
         out_shape=jax.ShapeDtypeStruct((CAND, D), BF16),
         in_specs=[anywhere] * 11,
-        out_specs=vmem,
+        out_specs=anywhere,
         scratch_shapes=[
+            pltpu.VMEM((CAND, D), BF16),
             pltpu.VMEM((1, CAND), jnp.int32),
             pltpu.VMEM((1, CAND), jnp.int32),
             pltpu.VMEM((1, 1), jnp.int32),
@@ -514,6 +523,7 @@
             pltpu.VMEM((2, 2, SIDE, SIDE, SHARD, 2 * QUARTER), BF16),
             pltpu.VMEM((PLANES, 1, 128), jnp.int32),
             pltpu.VMEM((PLANES, 1, 128), jnp.int32),
+            pltpu.VMEM((PIECES * CAND, PLANES * MESSAGE), BF16),
             pltpu.VMEM((256, 128), F32),
             pltpu.VMEM((len(GROUPS), 256, 128), BF16),
             pltpu.VMEM((PLANES, MESSAGE, 128), BF16),

time: 66 us -> 66 us (level); the launches traced: 65.4 us -> 64.7 us
  Pallas kernels: 63.2 us -> 62.5 us
    pallas_call x1, Pallas kernels: 63.2 us -> 62.5 us  [local(): pl.pallas_call(kernel, out_shape=jax.ShapeDtypeStruct((CAND, D), BF16), i...]
where the time goes in v4:
time: 66 us; the launch traced here: 64.7 us
  Pallas kernels  62.5 us (95%)
  local copies, waits for them, and re-layouts  1.54 us (2%)
  between operations  0.66 us (1%)
    pallas_call x1, Pallas kernels, local(): pl.pallas_call(kernel, out_shape=jax.ShapeDtypeStruct((CAND, D), BF16), i...  62.5 us
    unnamed x1, local copies, waits for them, and re-layouts  1.54 us

profile of v4, /device:TPU:1, one launch (start us, length us, event | category | flops | bytes accessed | tf_op | source)
XLA Modules:
  0.0 64.7 jit_solution(2349544369377008943)
XLA Ops:
  0.7 62.5 %layer.1 = bf16[48,1024]{1,0:T(8,128)(2,1)} custom-call(bf16[256,1024]{1,0:T(8,128)(2,1)} %table_hbm.1, s32[1,48]{1,0:T(1,128)} %bitcast.15, s32[1,48]{1,0:T(1,128)} %row_hbm.1, s32[1,1]{1,0:T(1,128)} %bitcast.8.counts_hbm, bf16[512,1024]{1,0:T(8,128)(2,1)} %bitcast.9, bf16[512,1024]{1,0:T(8,128)(2,1)} %bitcast.10, f32[1,1024]{1,0:T(1,128)} %bitcast.13, ...), custom_call_target="tpu_custom_call" | custom-call | tf_op jit(solution)/shard_map/layer/pallas_call | solution.py:506
  63.2 1.5 %copy.14 = bf16[1,48,1024]{2,1,0:T(8,128)(2,1)} copy(bf16[1,48,1024]{2,1,0:T(8,128)(2,1)} %bitcast.11) | data formatting | bytes 196608
